TPU v7x, 32 devices: a whole 2x2x4 slice. The times are simulated.
32 devices in a mesh: energy: 16 (over z, y, x), slab: 2 (over core).
Axes of the slice: x: 2, y: 2, z: 4, core: 2. Of those that a mesh axis runs over, the one named last changes fastest.
Arguments:
- green_local: bfloat16 [32, 2, 2, 512, 512], P('energy', 'slab'), may hold values from -2.5 to 2.5
- coupling: bfloat16 [2, 512, 512], P('slab', 'energy'), may hold values from -0.21875 to 0.21875
- masks: int32 [2, 4, 4], P('slab'), may hold values 0 or 1
- incident: bfloat16 [32, 2, 512, 2, 128], P('energy', 'slab'), may hold values from -3 to 3
- energy_index: int32 [32], P('energy'), may hold values from 0 to 255
Outputs:
- wave_field: bfloat16 [32, 2, 512, 2, 128], P('energy', 'slab')
- outflow: bfloat16 [32, 2, 512, 2, 128], P('energy', 'slab')
- density: float32 [2, 512, 2, 512], P('slab', 'energy')
All inputs are finite; a program needn't handle non-finite values. No bound on the sum of `masks` on one device may be relied on, other than what follows from the above.
Results may differ from a plain program's by a relative error of at most 0.027.
Values may be sent and summed in bfloat16 or wider, within the bound.
A program may use at most 64 MiB of HBM per device.

v0:
```python
import jax
import jax.numpy as jnp
from jax import lax
from jax.sharding import PartitionSpec as P


def shifted(block, axis, distance):
    devices = range(lax.axis_size(axis))
    route = [(i - distance, i) for i in devices if i - distance in devices]
    return lax.ppermute(block, axis, route)


def apply_green(green_block, vector):
    orbitals = green_block.shape[1]
    mode_count = vector.shape[2]
    product = jnp.dot(
        green_block.reshape(2 * orbitals, orbitals),
        vector.reshape(orbitals, 2 * mode_count),
        preferred_element_type=jnp.float32,
    )
    product = product.reshape(2, orbitals, 2, mode_count)
    real_part = product[0, :, 0] - product[1, :, 1]
    imag_part = product[0, :, 1] + product[1, :, 0]
    return jnp.stack([real_part, imag_part], axis=1).astype(jnp.bfloat16)


def couple_forward(matrix, vector):
    orbitals = vector.shape[0]
    product = jnp.dot(matrix, vector.reshape(orbitals, -1), preferred_element_type=jnp.float32)
    return product.reshape(vector.shape)


def couple_back(matrix, vector):
    orbitals = vector.shape[0]
    product = lax.dot_general(
        matrix,
        vector.reshape(orbitals, -1),
        (((0,), (0,)), ((), ())),
        preferred_element_type=jnp.float32,
    )
    return product.reshape(vector.shape)


def relax(green_block, source_here, left_term, matrix, right_wave):
    summed = (
        source_here.astype(jnp.float32)
        + left_term.astype(jnp.float32)
        + couple_forward(matrix, right_wave)
    )
    return apply_green(green_block, summed.astype(jnp.bfloat16))


def fermi(index_values, scale):
    exponent = (index_values.astype(jnp.float32) - 128.0) / 24.0
    return scale / (1.0 + jnp.exp(exponent))


def shards(green_local, coupling, masks, incident, energy_index):
    count_here = green_local.shape[0]
    orbitals = green_local.shape[3]
    mode_count = incident.shape[4]
    slab_count = lax.axis_size("slab")
    place_here = lax.axis_index("slab")
    energy_devices = lax.axis_size("energy")
    whole_rows = lax.all_gather(coupling, "energy", axis=1, tiled=True)[0]
    tile_size = orbitals // masks.shape[1]
    opened = jnp.repeat(jnp.repeat(masks[0], tile_size, axis=0), tile_size, axis=1)
    coupled = whole_rows * opened.astype(jnp.bfloat16)
    green_here = green_local[:, 0]
    source = incident[:, 0]
    first_waves = jax.vmap(apply_green)(green_here, source)
    right_start = shifted(first_waves, "slab", -1)
    step_count = slab_count * count_here

    def pick(step_index, position):
        energy = step_index // slab_count
        active = step_index % slab_count == position
        return (jnp.clip(energy, 0, count_here - 1), active)

    zero_wave = jnp.zeros((orbitals, 2, mode_count), jnp.bfloat16)
    left_terms = jnp.zeros((count_here, orbitals, 2, mode_count), jnp.bfloat16)

    def forward_step(step_index, loop_state):
        arrived = shifted(loop_state[0], "slab", 1)
        energy, active = pick(step_index, place_here)

        def forward_update(old_state):
            relaxed = relax(
                green_here[energy], source[energy], arrived, coupled, right_start[energy]
            )
            new_flux = couple_back(coupled, relaxed).astype(jnp.bfloat16)
            return (new_flux, old_state[1].at[energy].set(arrived))

        return lax.cond(active, forward_update, lambda old_state: old_state, loop_state)

    forward_state = lax.fori_loop(0, step_count, forward_step, (zero_wave, left_terms))
    left_terms = forward_state[1]
    wave_init = jnp.zeros((count_here, orbitals, 2, mode_count), jnp.bfloat16)

    def backward_step(step_index, loop_state):
        arrived = shifted(loop_state[0], "slab", -1)
        energy, active = pick(step_index, slab_count - 1 - place_here)

        def backward_update(old_state):
            relaxed = relax(
                green_here[energy], source[energy], left_terms[energy], coupled, arrived
            )
            return (relaxed, old_state[1].at[energy].set(relaxed))

        return lax.cond(active, backward_update, lambda old_state: old_state, loop_state)

    backward_state = lax.fori_loop(0, step_count, backward_step, (zero_wave, wave_init))
    wave_field = backward_state[1]
    outflow = jnp.einsum(
        "rc,erpk->ecpk", coupled, wave_field, preferred_element_type=jnp.float32
    ).astype(jnp.bfloat16)
    weights = fermi(energy_index, 4.0 / (count_here * energy_devices * mode_count))
    scaled = (wave_field.astype(jnp.float32) * weights[:, None, None, None]).astype(jnp.bfloat16)
    left_side = scaled.transpose(1, 0, 2, 3).reshape(orbitals, -1)
    right_real = wave_field.transpose(1, 0, 2, 3).reshape(orbitals, -1)
    right_imag = (
        jnp.stack([-wave_field[:, :, 1], wave_field[:, :, 0]], axis=2)
        .transpose(1, 0, 2, 3)
        .reshape(orbitals, -1)
    )
    real_part = lax.dot_general(
        left_side, right_real, (((1,), (1,)), ((), ())), preferred_element_type=jnp.float32
    )
    imag_part = lax.dot_general(
        left_side, right_imag, (((1,), (1,)), ((), ())), preferred_element_type=jnp.float32
    )
    density = lax.psum_scatter(
        jnp.stack([real_part, imag_part], axis=1), "energy", scatter_dimension=0, tiled=True
    )
    return (wave_field[:, None], outflow[:, None], density[None])


def solution(mesh):
    return jax.shard_map(
        shards,
        mesh=mesh,
        in_specs=(
            P("energy", "slab", None, None, None),
            P("slab", "energy", None),
            P("slab", None, None),
            P("energy", "slab", None, None, None),
            P("energy"),
        ),
        out_specs=(
            P("energy", "slab", None, None, None),
            P("energy", "slab", None, None, None),
            P("slab", "energy", None, None),
        ),
        check_vma=False,
    )
```

profile of v0, /device:TPU:0, one launch (start us, length us, event | category | flops | bytes accessed | tf_op | source)
XLA Modules:
  0.0 209.3 jit_solution(15088808454673919824)
XLA Ops:
  7.2 1.4 reshape_squeeze.7
  8.6 3.6 %fusion.49 = f32[2,1024,256]{2,1,0:T(8,128)} fusion(bf16[2,1024,512]{2,1,0:T(8,128)(2,1)} %bitcast.34, bf16[2,512,256]{2,1,0:T(8,128)(2,1)S(1)} %reshape_squeeze.7), kind=kOutput, calls=%fused_computation.72 | convolution fusion | flops 536870912 | bytes 4718592 | tf_op jit(solution)/shard_map/vmap()/dot_general | solution.py:16
  12.2 2.3 %reshape.303 = f32[2,2,512,2,128]{4,3,2,1,0:T(2,128)S(1)} reshape(f32[2,1024,256]{2,1,0:T(8,128)} %fusion.49) | data formatting | bytes 4194304 | tf_op jit(solution)/shard_map/vmap()/reshape | solution.py:21
  14.5 1.6 fusion.48
  18.2 45.5 %all_gather.3 = bf16[1,512,512]{2,1,0:T(8,128)(2,1)S(1)} all-gather(bf16[1,32,512]{2,1,0:T(8,128)(2,1)S(1)} %copy-done.1), channel_id=1, replica_groups=mesh['energy'=16,'slab'=2] {'energy'}, dimensions={1}, use_global_device_ids=true | all-gather | bytes 557056 | tf_op jit(solution)/shard_map/all_gather | solution.py:65
  64.4 1.6 copy.28
  66.1 24.3 %while.36 = (s32[]{:T(128)}, bf16[512,2,128]{0,2,1:T(8,128)(2,1)S(1)}, bf16[2,512,2,128]{1,3,2,0:T(8,128)(2,1)S(1)}, s32[]{:T(128)}, bf16[2,2,512,512]{3,2,1,0:T...) while((s32[]{:T(128)}, ...), condition=%wide.region_4.5_spmd, body=%wide.region_0.4_spmd.sunk | while | flops 538181632 | bytes 9700905 | solution.py:96
  68.5 4.5 %conditional.4 = ((bf16[512,2,128]{0,2,1:T(8,128)(2,1)S(1)}, bf16[2,512,2,128]{1,3,2,0:T(8,128)(2,1)S(1)})) conditional(s32[]{:T(128)} %convert_element_type.161, (bf16[512,2,128]{0,2,1:T(8,128)(2,1)S(1)}, bf16[2,512,2,128]{1,3,2,0:T(8,128)(2,1)S(1)}) %tuple.125, (s32[]{:T(128)}, bf16[2,2,512,512]{3,2,1,0:T(8,128)(2,1)}, ...), branch_computations={%region_1.1_spmd, %region_2.3_spmd} | conditional | flops 538181632 | bytes 8652028 | solution.py:94
  69.1 1.7 fusion
  75.5 6.8 %collective-permute-start = (bf16[512,2,128]{0,2,1:T(8,128)(2,1)S(1)}, bf16[512,2,128]{0,2,1:T(8,128)(2,1)S(1)}, u32[]{:S(2)}, u32[]{:S(2)}) collective-permute-start(bf16[512,2,128]{0,2,1:T(8,128)(2,1)S(1)} %get-tuple-element.889), channel_id=1, source_target_pairs={{0,1},{2,3},{4,5},{6,7},{8,9},{10,11},{12,13},{14,15},{16,17},{18,... | collective-permute-start | bytes 786440 | tf_op jit(solution)/shard_map/while/body/eval_jaxpr/ppermute | solution.py:10
  83.4 4.5 %conditional.4 = ((bf16[512,2,128]{0,2,1:T(8,128)(2,1)S(1)}, bf16[2,512,2,128]{1,3,2,0:T(8,128)(2,1)S(1)})) conditional(s32[]{:T(128)} %convert_element_type.161, (bf16[512,2,128]{0,2,1:T(8,128)(2,1)S(1)}, bf16[2,512,2,128]{1,3,2,0:T(8,128)(2,1)S(1)}) %tuple.125, (s32[]{:T(128)}, bf16[2,2,512,512]{3,2,1,0:T(8,128)(2,1)}, ...), branch_computations={%region_1.1_spmd, %region_2.3_spmd} | conditional | flops 538181632 | bytes 8652028 | solution.py:94
  83.9 1.7 fusion
  90.4 31.1 %while.37 = (s32[]{:T(128)}, bf16[512,2,128]{2,0,1:T(8,128)(2,1)S(1)}, bf16[2,512,2,128]{3,1,2,0:T(8,128)(2,1)S(1)}, s32[]{:T(128)}, bf16[2,2,512,512]{3,2,1,0:T...) while((s32[]{:T(128)}, ...), condition=%wide.region_9.10_spmd, body=%wide.region_5.9_spmd.sunk | while | flops 404357152 | bytes 7603749 | solution.py:112
  91.9 6.0 %collective-permute-done.1 = bf16[512,2,128]{0,2,1:T(8,128)(2,1)} collective-permute-done((bf16[512,2,128]{0,2,1:T(8,128)(2,1)S(1)}, bf16[512,2,128]{0,2,1:T(8,128)(2,1)}, u32[]{:S(2)}, u32[]{:S(2)}) %collective-permute-start.1) | collective-permute-done | bytes 262176 | tf_op jit(solution)/shard_map/while/body/eval_jaxpr/ppermute | solution.py:10
  99.4 4.9 %collective-permute-done.1 = bf16[512,2,128]{0,2,1:T(8,128)(2,1)} collective-permute-done((bf16[512,2,128]{0,2,1:T(8,128)(2,1)S(1)}, bf16[512,2,128]{0,2,1:T(8,128)(2,1)}, u32[]{:S(2)}, u32[]{:S(2)}) %collective-permute-start.1) | collective-permute-done | bytes 262176 | tf_op jit(solution)/shard_map/while/body/eval_jaxpr/ppermute | solution.py:10
  104.3 3.6 %conditional.5 = ((bf16[512,2,128]{2,0,1:T(8,128)(2,1)S(1)}, bf16[2,512,2,128]{3,1,2,0:T(8,128)(2,1)S(1)})) conditional(s32[]{:T(128)} %convert_element_type.162, (bf16[512,2,128]{2,0,1:T(8,128)(2,1)S(1)}, bf16[2,512,2,128]{3,1,2,0:T(8,128)(2,1)S(1)}) %tuple.128, (s32[]{:T(128)}, bf16[2,2,512,512]{3,2,1,0:T(8,128)(2,1)}, ...), branch_computations={%region_6.6_spmd, %region_7.8_spmd} | conditional | flops 404357152 | bytes 6030584 | solution.py:110
  104.3 2.1 fusion.20
  109.4 2.3 %collective-permute-done.1 = bf16[512,2,128]{0,2,1:T(8,128)(2,1)} collective-permute-done((bf16[512,2,128]{0,2,1:T(8,128)(2,1)S(1)}, bf16[512,2,128]{0,2,1:T(8,128)(2,1)}, u32[]{:S(2)}, u32[]{:S(2)}) %collective-permute-start.1) | collective-permute-done | bytes 262176 | tf_op jit(solution)/shard_map/while/body/eval_jaxpr/ppermute | solution.py:10
  113.1 4.9 %collective-permute-done.1 = bf16[512,2,128]{0,2,1:T(8,128)(2,1)} collective-permute-done((bf16[512,2,128]{0,2,1:T(8,128)(2,1)S(1)}, bf16[512,2,128]{0,2,1:T(8,128)(2,1)}, u32[]{:S(2)}, u32[]{:S(2)}) %collective-permute-start.1) | collective-permute-done | bytes 262176 | tf_op jit(solution)/shard_map/while/body/eval_jaxpr/ppermute | solution.py:10
  118.0 3.6 %conditional.5 = ((bf16[512,2,128]{2,0,1:T(8,128)(2,1)S(1)}, bf16[2,512,2,128]{3,1,2,0:T(8,128)(2,1)S(1)})) conditional(s32[]{:T(128)} %convert_element_type.162, (bf16[512,2,128]{2,0,1:T(8,128)(2,1)S(1)}, bf16[2,512,2,128]{3,1,2,0:T(8,128)(2,1)S(1)}) %tuple.128, (s32[]{:T(128)}, bf16[2,2,512,512]{3,2,1,0:T(8,128)(2,1)}, ...), branch_computations={%region_6.6_spmd, %region_7.8_spmd} | conditional | flops 404357152 | bytes 6030584 | solution.py:110
  118.0 2.0 fusion.20
  122.6 1.6 pad_maximum_fusion.2
  127.1 73.8 %reduce-scatter.2.cloned.1.call-done = f32[32,2,512]{2,0,1:T(8,128)} async-done(((f32[512,2,512]{2,0,1:T(8,128)}), f32[32,2,512]{2,0,1:T(8,128)}) %reduce-scatter.2.cloned.1.call-update) | async-done | bytes 131088 | tf_op jit(solution)/shard_map/reduce_scatter | solution.py:132
  200.8 1.7 copy.32
  (79 shorter events, 29.4 us)
Async XLA Ops:
  7.2 193.7 %reduce-scatter.2.cloned.1.call-start = ((), (), s32[]{:S(2)}) async-start(), calls=%async_computation.1 | async-start | bytes 2228224 | tf_op jit(solution)/shard_map/reduce_scatter | solution.py:132
  16.1 1.5 copy-start.4
  16.2 1.5 copy-start.5
  16.2 1.5 copy-start
  16.2 2.0 copy-start.1
  16.4 48.0 %collective-permute-start.2 = (bf16[2,512,2,128]{3,1,0,2:T(8,128)(2,1)S(1)}, bf16[2,512,2,128]{3,1,0,2:T(8,128)(2,1)}, u32[]{:S(2)}, u32[]{:S(2)}) collective-permute-start(bf16[2,512,2,128]{3,1,0,2:T(8,128)(2,1)S(1)} %pad_maximum_fusion.3), channel_id=1, source_target_pairs={{1,0},{3,2},{5,4},{7,6},{9,8},{11,10},{13,12},{15,14},{17,16},{19,... | collective-permute-start | bytes 1572872 | tf_op jit(solution)/shard_map/ppermute | solution.py:10
  66.1 2.4 %collective-permute-start = (bf16[512,2,128]{0,2,1:T(8,128)(2,1)S(1)}, bf16[512,2,128]{0,2,1:T(8,128)(2,1)S(1)}, u32[]{:S(2)}, u32[]{:S(2)}) collective-permute-start(bf16[512,2,128]{0,2,1:T(8,128)(2,1)S(1)} %get-tuple-element.889), channel_id=1, source_target_pairs={{0,1},{2,3},{4,5},{6,7},{8,9},{10,11},{12,13},{14,15},{16,17},{18,... | collective-permute-start | bytes 786440 | tf_op jit(solution)/shard_map/while/body/eval_jaxpr/ppermute | solution.py:10
  70.8 0.7 copy-start.2
  73.0 2.4 %collective-permute-start = (bf16[512,2,128]{0,2,1:T(8,128)(2,1)S(1)}, bf16[512,2,128]{0,2,1:T(8,128)(2,1)S(1)}, u32[]{:S(2)}, u32[]{:S(2)}) collective-permute-start(bf16[512,2,128]{0,2,1:T(8,128)(2,1)S(1)} %get-tuple-element.889), channel_id=1, source_target_pairs={{0,1},{2,3},{4,5},{6,7},{8,9},{10,11},{12,13},{14,15},{16,17},{18,... | collective-permute-start | bytes 786440 | tf_op jit(solution)/shard_map/while/body/eval_jaxpr/ppermute | solution.py:10
  75.5 7.9 %collective-permute-start = (bf16[512,2,128]{0,2,1:T(8,128)(2,1)S(1)}, bf16[512,2,128]{0,2,1:T(8,128)(2,1)S(1)}, u32[]{:S(2)}, u32[]{:S(2)}) collective-permute-start(bf16[512,2,128]{0,2,1:T(8,128)(2,1)S(1)} %get-tuple-element.889), channel_id=1, source_target_pairs={{0,1},{2,3},{4,5},{6,7},{8,9},{10,11},{12,13},{14,15},{16,17},{18,... | collective-permute-start | bytes 786440 | tf_op jit(solution)/shard_map/while/body/eval_jaxpr/ppermute | solution.py:10
  85.6 0.7 copy-start.2
  87.9 2.4 %collective-permute-start = (bf16[512,2,128]{0,2,1:T(8,128)(2,1)S(1)}, bf16[512,2,128]{0,2,1:T(8,128)(2,1)S(1)}, u32[]{:S(2)}, u32[]{:S(2)}) collective-permute-start(bf16[512,2,128]{0,2,1:T(8,128)(2,1)S(1)} %get-tuple-element.889), channel_id=1, source_target_pairs={{0,1},{2,3},{4,5},{6,7},{8,9},{10,11},{12,13},{14,15},{16,17},{18,... | collective-permute-start | bytes 786440 | tf_op jit(solution)/shard_map/while/body/eval_jaxpr/ppermute | solution.py:10
  90.6 7.3 %collective-permute-start.1 = (bf16[512,2,128]{0,2,1:T(8,128)(2,1)S(1)}, bf16[512,2,128]{0,2,1:T(8,128)(2,1)}, u32[]{:S(2)}, u32[]{:S(2)}) collective-permute-start(bf16[512,2,128]{0,2,1:T(8,128)(2,1)S(1)} %copy.53), channel_id=1, source_target_pairs={{1,0},{3,2},{5,4},{7,6},{9,8},{11,10},{13,12},{15,14},{17,16},{19,... | collective-permute-start | bytes 786440 | tf_op jit(solution)/shard_map/while/body/eval_jaxpr/ppermute | solution.py:10
  98.1 6.2 %collective-permute-start.1 = (bf16[512,2,128]{0,2,1:T(8,128)(2,1)S(1)}, bf16[512,2,128]{0,2,1:T(8,128)(2,1)}, u32[]{:S(2)}, u32[]{:S(2)}) collective-permute-start(bf16[512,2,128]{0,2,1:T(8,128)(2,1)S(1)} %copy.53), channel_id=1, source_target_pairs={{1,0},{3,2},{5,4},{7,6},{9,8},{11,10},{13,12},{15,14},{17,16},{19,... | collective-permute-start | bytes 786440 | tf_op jit(solution)/shard_map/while/body/eval_jaxpr/ppermute | solution.py:10
  104.3 2.1 %copy-start.3 = (s32[4]{0:T(128)S(1)}, s32[4]{0:T(128)}, u32[]{:S(2)}) copy-start(s32[4]{0:T(128)} %constant.216.clone) | copy-start | bytes 52 | tf_op jit(solution)/shard_map/while/body/eval_jaxpr/cond
  108.1 3.6 %collective-permute-start.1 = (bf16[512,2,128]{0,2,1:T(8,128)(2,1)S(1)}, bf16[512,2,128]{0,2,1:T(8,128)(2,1)}, u32[]{:S(2)}, u32[]{:S(2)}) collective-permute-start(bf16[512,2,128]{0,2,1:T(8,128)(2,1)S(1)} %copy.53), channel_id=1, source_target_pairs={{1,0},{3,2},{5,4},{7,6},{9,8},{11,10},{13,12},{15,14},{17,16},{19,... | collective-permute-start | bytes 786440 | tf_op jit(solution)/shard_map/while/body/eval_jaxpr/ppermute | solution.py:10
  111.8 6.2 %collective-permute-start.1 = (bf16[512,2,128]{0,2,1:T(8,128)(2,1)S(1)}, bf16[512,2,128]{0,2,1:T(8,128)(2,1)}, u32[]{:S(2)}, u32[]{:S(2)}) collective-permute-start(bf16[512,2,128]{0,2,1:T(8,128)(2,1)S(1)} %copy.53), channel_id=1, source_target_pairs={{1,0},{3,2},{5,4},{7,6},{9,8},{11,10},{13,12},{15,14},{17,16},{19,... | collective-permute-start | bytes 786440 | tf_op jit(solution)/shard_map/while/body/eval_jaxpr/ppermute | solution.py:10
  118.0 2.1 copy-start.3
Sparse Core Ops, SparseCore 0:
  124.3 76.4 reduce-scatter.1
where the time goes:
time: 210 us; the launch traced here: 209 us
  waiting for transfers between devices  96.3 us (46%)
  blocking collectives  45.5 us (22%)
  starting transfers between devices  17.2 us (8%)
  between operations  14.2 us (7%)
  matrix products  13.8 us (7%)
  local copies, waits for them, and re-layouts  13.6 us (6%)
  other arithmetic  8.21 us (4%)
    reduce_scatter x1, waiting for transfers between devices, shards(): lax.psum_scatter(jnp.stack([real_part, imag_part], axis=1), 'energy', sca...  73.8 us
    all_gather x1, blocking collectives, shards(): whole_rows = lax.all_gather(coupling, 'energy', axis=1, tiled=True)[0]  45.5 us
    ppermute x9, waiting for transfers between devices, shifted(): return lax.ppermute(block, axis, route)  22.5 us
    ppermute x9, starting transfers between devices, shifted(): return lax.ppermute(block, axis, route)  17.2 us
    dot_general x5, matrix products, apply_green(): jnp.dot(green_block.reshape(2 * orbitals, orbitals), vector.reshape(orbit...  11.1 us
  transfers between devices with their start and end apart: 10, of which 9 were waited for; matrix products, arithmetic and copies ran while one was open for 2% of the time, Pallas kernels for 0%

commit v1 on v0

v1 whole, which is shorter than its diff:
```python
import functools

import jax
import jax.numpy as jnp
from jax import lax
from jax.experimental import pallas as pl
from jax.experimental.pallas import tpu as pltpu
from jax.sharding import PartitionSpec as P

MESH = pl.DeviceIdType.MESH
BF16 = jnp.bfloat16
F32 = jnp.float32


def dot(a, b):
    return jnp.dot(a, b, preferred_element_type=F32)


def dot_nt(a, b):
    return lax.dot_general(a, b, (((1,), (1,)), ((), ())), preferred_element_type=F32)


def turned(x):
    half = x.shape[1] // 2
    return jnp.concatenate([-x[:, half:], x[:, :half]], axis=1)


def gather_orders(k):
    first = list(range(k - 1, -1, -1))
    return [first, first[:-2] + first[-2:][::-1]]


def scatter_orders(k):
    first = list(range(k))
    return [first, first[:2][::-1] + first[2:]]


def kernel(n, slabs, count, scale, index_ref, mask_ref, green_ref, source_ref, coupling_ref,
           wave_ref, outflow_ref, density_ref, s):
    k = n.bit_length() - 1
    rows, orbitals = coupling_ref.shape
    me = lax.axis_index("energy")
    slab = lax.axis_index("slab")
    bit = [(me // 2**b) % 2 for b in range(k)]
    partner = [me + (1 - 2 * bit[b]) * 2**b for b in range(k)]
    gathered = s["gathered"]
    gathered[tuple(bit[b] for b in range(k - 1, -1, -1))] = coupling_ref[...]

    barrier = pltpu.get_barrier_semaphore()
    for b in range(k):
        pl.semaphore_signal(barrier, inc=1, device_id={"energy": partner[b]}, device_id_type=MESH)

    @pl.when(slab > 0)
    def _():
        pl.semaphore_signal(barrier, inc=1, device_id={"slab": slab - 1}, device_id_type=MESH)

    @pl.when(slab < slabs - 1)
    def _():
        pl.semaphore_signal(barrier, inc=1, device_id={"slab": slab + 1}, device_id_type=MESH)

    neighbours = jnp.minimum(slab, 1) + jnp.minimum(slabs - 1 - slab, 1)
    pl.semaphore_wait(barrier, k + neighbours)

    def green(e, x):
        return (dot(green_ref[e, 0], x) + dot(green_ref[e, 1], turned(x))).astype(BF16)

    def slab_copy(name, e, src, target):
        return pltpu.make_async_remote_copy(
            src_ref=src.at[e], dst_ref=s[name].at[e],
            send_sem=s[name + "_send"].at[e], recv_sem=s[name + "_recv"].at[e],
            device_id={"slab": target}, device_id_type=MESH,
        )

    def start_copy(e):
        return slab_copy("start", e, s["first"], slab - 1)

    def flux_copy(e):
        return slab_copy("flux", e, s["flux_out"], slab + 1)

    def wave_copy(e):
        return slab_copy("right_wave", e, wave_ref, slab - 1)

    def gather_copy(h, i):
        order = gather_orders(k)[h]
        b = order[i]
        width = orbitals // 2
        place = tuple(slice(None) if c in order[:i] else bit[c] for c in range(k - 1, -1, -1))
        block = gathered.at[place + (slice(None), pl.ds(h * width, width))]
        return pltpu.make_async_remote_copy(
            src_ref=block, dst_ref=block,
            send_sem=s["gather_send"].at[h, i], recv_sem=s["gather_recv"].at[h, i],
            device_id={"energy": partner[b]}, device_id_type=MESH,
        )

    def scatter_place(h, i, own):
        order = scatter_orders(k)[h]
        left = [c for c in range(k - 1, -1, -1) if c not in order[:i]]
        b = order[i]
        return tuple((bit[c] if own else 1 - bit[c]) if c == b else slice(None) for c in left)

    def scatter_copy(h, i):
        b = scatter_orders(k)[h][i]
        return pltpu.make_async_remote_copy(
            src_ref=s["part"][h][i].at[scatter_place(h, i, False)], dst_ref=s["part_in"][h][i],
            send_sem=s["scatter_send"].at[h, i], recv_sem=s["scatter_recv"].at[h, i],
            device_id={"energy": partner[b]}, device_id_type=MESH,
        )

    for h in range(2):
        gather_copy(h, 0).start()

    @pl.when(slab > 0)
    def _():
        for e in range(count):
            s["first"][e] = green(e, source_ref[e])
            start_copy(e).start()

    for i in range(k):
        for h in range(2):
            gather_copy(h, i).wait_recv()
            if i + 1 < k:
                gather_copy(h, i + 1).start()

    whole = gathered[...].astype(F32).reshape(orbitals, orbitals)
    blocks = mask_ref.shape[0]
    tile = orbitals // blocks
    for i in range(blocks):
        for j in range(blocks):
            block = whole[i * tile:(i + 1) * tile, j * tile:(j + 1) * tile] * mask_ref[i, j].astype(F32)
            s["coupled"][i * tile:(i + 1) * tile, j * tile:(j + 1) * tile] = block.astype(BF16)
            s["coupled_t"][j * tile:(j + 1) * tile, i * tile:(i + 1) * tile] = block.T.astype(BF16)

    def sweep(has_left, has_right):
        for e in range(count):
            total = source_ref[e].astype(F32)
            if has_right:
                start_copy(e).wait_recv()
                total = total + dot(s["coupled"][...], s["start"][e])
            if has_left:
                flux_copy(e).wait_recv()
                total = total + s["flux"][e].astype(F32)
            forward = green(e, total.astype(BF16))
            if has_right:
                s["flux_out"][e] = dot(s["coupled_t"][...], forward).astype(BF16)
                flux_copy(e).start()
            else:
                wave_ref[e] = forward
                if has_left:
                    wave_copy(e).start()
        if has_right:
            for e in range(count):
                wave_copy(e).wait_recv()
                total = source_ref[e].astype(F32) + dot(s["coupled"][...], s["right_wave"][e])
                if has_left:
                    total = total + s["flux"][e].astype(F32)
                wave_ref[e] = green(e, total.astype(BF16))
                if has_left:
                    wave_copy(e).start()

    @pl.when(slab == 0)
    def _():
        sweep(False, slabs > 1)

    if slabs > 2:
        @pl.when((slab > 0) & (slab < slabs - 1))
        def _():
            sweep(True, True)

    if slabs > 1:
        @pl.when(slab == slabs - 1)
        def _():
            sweep(True, False)

    scaled = []
    for e in range(count):
        index = jnp.full((1, wave_ref.shape[2]), index_ref[e].astype(F32), F32)
        weight = scale / (1.0 + jnp.exp((index - 128.0) / 24.0))
        scaled.append((wave_ref[e].astype(F32) * weight).astype(BF16))
    left_side = jnp.concatenate(scaled, axis=1)
    for h in range(2):
        waves = [turned(wave_ref[e]) if h else wave_ref[e] for e in range(count)]
        part = dot_nt(left_side, jnp.concatenate(waves, axis=1))
        s["part"][h][0][...] = part.reshape((2,) * k + (rows, orbitals)).astype(BF16)
        scatter_copy(h, 0).start()

    for e in range(count):
        outflow_ref[e] = dot(s["coupled_t"][...], wave_ref[e]).astype(BF16)

    for i in range(k):
        for h in range(2):
            scatter_copy(h, i).wait_recv()
            total = s["part"][h][i][scatter_place(h, i, True)].astype(F32) + s["part_in"][h][i][...].astype(F32)
            if i + 1 < k:
                s["part"][h][i + 1][...] = total.astype(BF16)
                scatter_copy(h, i + 1).start()
            else:
                density_ref[:, h * orbitals:(h + 1) * orbitals] = total

    for h in range(2):
        for i in range(k):
            gather_copy(h, i).wait_send()
            scatter_copy(h, i).wait_send()

    @pl.when(slab > 0)
    def _():
        for e in range(count):
            start_copy(e).wait_send()
            wave_copy(e).wait_send()

    @pl.when(slab < slabs - 1)
    def _():
        for e in range(count):
            flux_copy(e).wait_send()


def shards(green_local, coupling, masks, incident, energy_index):
    count = green_local.shape[0]
    orbitals = green_local.shape[3]
    modes = incident.shape[4]
    rows = coupling.shape[1]
    slabs = lax.axis_size("slab")
    n = lax.axis_size("energy")
    k = n.bit_length() - 1
    wave = (count, orbitals, 2 * modes)
    scratch = {
        "gathered": pltpu.VMEM((2,) * k + (rows, orbitals), BF16),
        "coupled": pltpu.VMEM((orbitals, orbitals), BF16),
        "coupled_t": pltpu.VMEM((orbitals, orbitals), BF16),
        "first": pltpu.VMEM(wave, BF16),
        "flux_out": pltpu.VMEM(wave, BF16),
        "gather_send": pltpu.SemaphoreType.DMA((2, k)),
        "gather_recv": pltpu.SemaphoreType.DMA((2, k)),
        "scatter_send": pltpu.SemaphoreType.DMA((2, k)),
        "scatter_recv": pltpu.SemaphoreType.DMA((2, k)),
        "part": [[pltpu.VMEM((2,) * (k - i) + (rows, orbitals), BF16) for i in range(k)] for h in range(2)],
        "part_in": [[pltpu.VMEM((2,) * (k - i - 1) + (rows, orbitals), BF16) for i in range(k)] for h in range(2)],
    }
    for name in ("start", "flux", "right_wave"):
        scratch[name] = pltpu.VMEM(wave, BF16)
        scratch[name + "_send"] = pltpu.SemaphoreType.DMA((count,))
        scratch[name + "_recv"] = pltpu.SemaphoreType.DMA((count,))
    vmem = pl.BlockSpec(memory_space=pltpu.VMEM)
    smem = pl.BlockSpec(memory_space=pltpu.SMEM)
    wave_field, outflow, density = pl.pallas_call(
        functools.partial(kernel, n, slabs, count, 4.0 / (count * n * modes)),
        out_shape=(
            jax.ShapeDtypeStruct(wave, BF16),
            jax.ShapeDtypeStruct(wave, BF16),
            jax.ShapeDtypeStruct((rows, 2 * orbitals), F32),
        ),
        in_specs=[smem, smem, vmem, vmem, vmem],
        out_specs=(vmem, vmem, vmem),
        scratch_shapes=[scratch],
        compiler_params=pltpu.CompilerParams(
            collective_id=0, has_side_effects=True, vmem_limit_bytes=48 * 2**20
        ),
        name="sweep_and_density",
    )(energy_index, masks[0], green_local[:, 0], incident[:, 0].reshape(wave), coupling[0])
    shape = (count, 1, orbitals, 2, modes)
    return (wave_field.reshape(shape), outflow.reshape(shape), density.reshape(1, rows, 2, orbitals))


def solution(mesh):
    return jax.shard_map(
        shards,
        mesh=mesh,
        in_specs=(
            P("energy", "slab", None, None, None),
            P("slab", "energy", None),
            P("slab", None, None),
            P("energy", "slab", None, None, None),
            P("energy"),
        ),
        out_specs=(
            P("energy", "slab", None, None, None),
            P("energy", "slab", None, None, None),
            P("slab", "energy", None, None),
        ),
        check_vma=False,
    )
```

time: 210 us -> 54.6 us (0.26)
  waiting for transfers between devices: 96.3 us -> 0 us
  Pallas kernels: 0 us -> 46 us
  blocking collectives: 45.5 us -> 0 us
  starting transfers between devices: 17.2 us -> 0 us
  matrix products: 13.8 us -> 0 us
  between operations: 14.2 us -> 0.65 us
  other arithmetic: 8.21 us -> 0 us
  local copies, waits for them, and re-layouts: 13.6 us -> 7.65 us
    reduce_scatter x1 -> x0, waiting for transfers between devices: 73.8 us -> none  [shards(): lax.psum_scatter(jnp.stack([real_part, imag_part], axis=1), 'energy', sca...]
    pallas_call x0 -> x1, Pallas kernels: none -> 46 us  [shards(): pl.pallas_call(functools.partial(kernel, n, slabs, count, 4.0 / (count *...]
    all_gather x1 -> x0, blocking collectives: 45.5 us -> none  [shards(): whole_rows = lax.all_gather(coupling, 'energy', axis=1, tiled=True)[0]]
    ppermute x9 -> x0, waiting for transfers between devices: 22.5 us -> none  [shifted(): return lax.ppermute(block, axis, route)]
    ppermute x9 -> x0, starting transfers between devices: 17.2 us -> none  [shifted(): return lax.ppermute(block, axis, route)]
    dot_general x12 -> x0, matrix products: 13.8 us -> none  [the longest x5 11.1 us: apply_green(): jnp.dot(green_block.reshape(2 * orbitals, orbitals), vector.reshape(orbit...]
    another operation x12 -> x0, other arithmetic: 4.88 us -> none
    scatter x4 -> x0, other arithmetic: 2.93 us -> none  [the longest x2 1.52 us: forward_update(): return (new_flux, old_state[1].at[energy].set(arrived))]
  transfers between devices with their start and end apart: 10 -> 0, of which waited for: 9 -> 0; matrix products, arithmetic and copies ran while one was open for 2% -> 0% of each run, Pallas kernels for 0% -> 0%
where the time goes in v1:
time: 54.6 us; the launch traced here: 54.3 us
  Pallas kernels  46 us (84%)
  local copies, waits for them, and re-layouts  7.65 us (14%)
  between operations  0.65 us (1%)
    pallas_call x1, Pallas kernels, shards(): pl.pallas_call(functools.partial(kernel, n, slabs, count, 4.0 / (count *...  46 us
    unnamed x8, local copies, waits for them, and re-layouts  3.68 us
    another operation x1, local copies, waits for them, and re-layouts, shards(): incident[:, 0].reshape(wave)  1.37 us

profile of v1, /device:TPU:0, one launch (start us, length us, event | category | flops | bytes accessed | tf_op | source)
XLA Modules:
  0.0 54.3 jit_solution(17815936513015412537)
XLA Ops:
  0.6 1.4 %reshape_squeeze.3.source_ref = bf16[2,512,256]{2,1,0:T(8,128)(2,1)S(1)} reshape(bf16[2,1,512,2,128]{4,3,2,1,0:T(2,128)(2,1)} %param.8) | data formatting | bytes 1048576 | tf_op jit(solution)/shard_map/reshape;squeeze | solution.py:258
  2.0 0.0 copy-start
  2.0 1.6 %copy-done = bf16[2,1,2,512,512]{4,3,2,1,0:T(8,128)(2,1)S(1)} copy-done((bf16[2,1,2,512,512]{4,3,2,1,0:T(8,128)(2,1)S(1)}, bf16[2,1,2,512,512]{4,3,2,1,0:T(8,128)(2,1)}, u32[]{:S(2)}) %copy-start) | copy-done | bytes 2097176
  3.6 0.0 copy-start.1
  3.6 0.8 %copy-done.1 = bf16[1,32,512]{2,1,0:T(8,128)(2,1)S(1)} copy-done((bf16[1,32,512]{2,1,0:T(8,128)(2,1)S(1)}, bf16[1,32,512]{2,1,0:T(8,128)(2,1)}, u32[]{:S(2)}) %copy-start.1) | copy-done | bytes 32792
  4.4 0.0 copy-start.2
  4.4 0.7 %copy-done.2 = s32[1,4,4]{2,1,0:T(4,128)S(1)} copy-done((s32[1,4,4]{2,1,0:T(4,128)S(1)}, s32[1,4,4]{2,1,0:T(4,128)}, u32[]{:S(2)}) %copy-start.2) | copy-done | bytes 88
  5.0 0.0 copy-start.3
  5.0 0.7 %copy-done.3 = s32[2]{0:T(128)S(1)} copy-done((s32[2]{0:T(128)S(1)}, s32[2]{0:T(128)}, u32[]{:S(2)}) %copy-start.3) | copy-done | bytes 32
  5.7 46.0 %sweep_and_density.1 = (bf16[2,512,256]{2,1,0:T(8,128)(2,1)S(1)}, bf16[2,512,256]{2,1,0:T(8,128)(2,1)S(1)}, f32[32,1024]{1,0:T(8,128)S(1)}) custom-call(s32[2]{0:T(128)S(1)} %copy-done.3, s32[4,4]{1,0:T(4,128)S(1)} %bitcast.7, bf16[2,2,512,512]{3,2,1,0:T(8,128)(2,1)S(1)} %bitcast.5, bf16[2,512,256]{2,1,0:T(8,128)(2,1)S(1)} %reshape_squeeze.3.source_ref, ...), custom_call_target="tpu_custom_call" | custom-call | tf_op jit(solution)/shard_map/sweep_and_density/pallas_call | solution.py:244
  51.7 0.9 %reshape.15 = bf16[2,1,512,2,128]{4,3,2,0,1:T(2,128)(2,1)} reshape(bf16[2,512,256]{2,1,0:T(8,128)(2,1)S(1)} %get-tuple-element.6) | data formatting | bytes 1048576 | tf_op jit(solution)/shard_map/reshape | solution.py:260
  52.7 0.8 %reshape.17 = f32[1,32,2,512]{3,2,1,0:T(2,128)} reshape(f32[32,1024]{1,0:T(8,128)S(1)} %get-tuple-element.8) | data formatting | bytes 262144 | tf_op jit(solution)/shard_map/reshape | solution.py:260
  53.4 0.9 %reshape.16 = bf16[2,1,512,2,128]{4,3,2,0,1:T(2,128)(2,1)} reshape(bf16[2,512,256]{2,1,0:T(8,128)(2,1)S(1)} %get-tuple-element.7) | data formatting | bytes 1048576 | tf_op jit(solution)/shard_map/reshape | solution.py:260
Async XLA Ops:
  2.0 1.6 %copy-start = (bf16[2,1,2,512,512]{4,3,2,1,0:T(8,128)(2,1)S(1)}, bf16[2,1,2,512,512]{4,3,2,1,0:T(8,128)(2,1)}, u32[]{:S(2)}) copy-start(bf16[2,1,2,512,512]{4,3,2,1,0:T(8,128)(2,1)} %param.5) | copy-start | bytes 6291460
  3.6 0.8 %copy-start.1 = (bf16[1,32,512]{2,1,0:T(8,128)(2,1)S(1)}, bf16[1,32,512]{2,1,0:T(8,128)(2,1)}, u32[]{:S(2)}) copy-start(bf16[1,32,512]{2,1,0:T(8,128)(2,1)} %param.6) | copy-start | bytes 98308
  4.4 0.7 %copy-start.2 = (s32[1,4,4]{2,1,0:T(4,128)S(1)}, s32[1,4,4]{2,1,0:T(4,128)}, u32[]{:S(2)}) copy-start(s32[1,4,4]{2,1,0:T(4,128)} %param.7) | copy-start | bytes 196
  5.0 0.7 %copy-start.3 = (s32[2]{0:T(128)S(1)}, s32[2]{0:T(128)}, u32[]{:S(2)}) copy-start(s32[2]{0:T(128)} %index_ref.1) | copy-start | bytes 28

commit v2 on v1

v2 whole, which is shorter than its diff:
```python
import functools

import jax
import jax.numpy as jnp
from jax import lax
from jax.experimental import pallas as pl
from jax.experimental.pallas import tpu as pltpu
from jax.sharding import PartitionSpec as P

MESH = pl.DeviceIdType.MESH
BF16 = jnp.bfloat16
F32 = jnp.float32


def dot(a, b):
    return jnp.dot(a, b, preferred_element_type=F32)


def dot_nt(a, b):
    return lax.dot_general(a, b, (((1,), (1,)), ((), ())), preferred_element_type=F32)


def turned(x):
    half = x.shape[1] // 2
    return jnp.concatenate([-x[:, half:], x[:, :half]], axis=1)


def build(n, slabs, count, scale, index_hbm, mask_hbm, green_hbm, incident_hbm, coupling_hbm,
          wave_ref, outflow_ref, density_ref, s):
    layers = n // 4
    _, rows, orbitals = coupling_hbm.shape
    modes = incident_hbm.shape[4]
    me = lax.axis_index("energy")
    slab = lax.axis_index("slab")
    z, y, x = me // 4, (me // 2) % 2, me % 2
    across = {"x": me + 1 - 2 * x, "y": me + 2 - 4 * y}

    def layer_peer(j):
        return ((z + j) % layers) * 4 + me % 4

    gathered = s["gathered"]
    source_ref = s["source"]
    own = gathered.at[z, y, x]
    local = [pltpu.make_async_copy(coupling_hbm.at[0], own, s["local"].at[0])]
    local.append(pltpu.make_async_copy(incident_hbm.at[:, 0], s["raw"], s["local"].at[1]))
    local.append(pltpu.make_async_copy(index_hbm, s["index"], s["local"].at[2]))
    local.append(pltpu.make_async_copy(mask_hbm.at[0], s["mask"], s["local"].at[3]))
    for copy in local:
        copy.start()
    green_copies = []
    for e in range(count):
        for p in range(2):
            copy = pltpu.make_async_copy(
                green_hbm.at[e, 0, p], s["green"].at[e, :, pl.ds(p * orbitals, orbitals)], s["green_in"].at[e, p]
            )
            copy.start()
            green_copies.append(copy)

    barrier = pltpu.get_barrier_semaphore()
    for peer in [across["x"], across["y"]] + [layer_peer(j) for j in range(1, layers)]:
        pl.semaphore_signal(barrier, inc=1, device_id={"energy": peer}, device_id_type=MESH)

    @pl.when(slab > 0)
    def _():
        pl.semaphore_signal(barrier, inc=1, device_id={"slab": slab - 1}, device_id_type=MESH)

    @pl.when(slab < slabs - 1)
    def _():
        pl.semaphore_signal(barrier, inc=1, device_id={"slab": slab + 1}, device_id_type=MESH)

    local[1].wait()
    for e in range(count):
        source_ref[e] = jnp.concatenate([s["raw"][e, :, 0, :], s["raw"][e, :, 1, :]], axis=1)
    for copy in [local[0]] + local[2:] + green_copies:
        copy.wait()
    neighbours = jnp.minimum(slab, 1) + jnp.minimum(slabs - 1 - slab, 1)
    pl.semaphore_wait(barrier, layers + 1 + neighbours)

    def green(e, v):
        return dot(s["green"][e], jnp.concatenate([v, turned(v)], axis=0)).astype(BF16)

    def slab_copy(name, e, src, target):
        return pltpu.make_async_remote_copy(
            src_ref=src.at[e], dst_ref=s[name].at[e],
            send_sem=s[name + "_send"].at[e], recv_sem=s[name + "_recv"].at[e],
            device_id={"slab": target}, device_id_type=MESH,
        )

    def start_copy(e):
        return slab_copy("start", e, s["first"], slab - 1)

    def flux_copy(e):
        return slab_copy("flux", e, s["flux_out"], slab + 1)

    def wave_copy(e):
        return slab_copy("right_wave", e, wave_ref, slab - 1)

    def gather_layer(j):
        return pltpu.make_async_remote_copy(
            src_ref=own, dst_ref=own,
            send_sem=s["layer_send"].at[j], recv_sem=s["layer_recv"].at[j],
            device_id={"energy": layer_peer(j)}, device_id_type=MESH,
        )

    def gather_across(h, i):
        axis = ("yx", "xy")[h][i]
        columns = pl.ds(h * (orbitals // 2), orbitals // 2)
        yy = y if axis == "y" or i == 0 else slice(None)
        xx = x if axis == "x" or i == 0 else slice(None)
        block = gathered.at[:, yy, xx, :, columns]
        return pltpu.make_async_remote_copy(
            src_ref=block, dst_ref=block,
            send_sem=s["across_send"].at[h, i], recv_sem=s["across_recv"].at[h, i],
            device_id={"energy": across[axis]}, device_id_type=MESH,
        )

    def gather_0():
        for j in range(1, layers):
            gather_layer(j).start()

    def gather_1():
        for j in range(1, layers):
            gather_layer(j).wait_recv()
        for h in range(2):
            gather_across(h, 0).start()

    def gather_2():
        for h in range(2):
            gather_across(h, 0).wait_recv()
            gather_across(h, 1).start()

    def gather_3():
        for h in range(2):
            gather_across(h, 1).wait_recv()
        whole = gathered[...].astype(F32).reshape(orbitals, orbitals)
        blocks = s["mask"].shape[0]
        tile = orbitals // blocks
        for i in range(blocks):
            for j in range(blocks):
                block = whole[i * tile:(i + 1) * tile, j * tile:(j + 1) * tile] * s["mask"][i, j].astype(F32)
                s["coupled"][i * tile:(i + 1) * tile, j * tile:(j + 1) * tile] = block.astype(BF16)

    def transpose_coupled():
        s["coupled_t"][...] = s["coupled"][...].T

    def send_first():
        for e in range(count):
            s["first"][e] = green(e, source_ref[e])
            start_copy(e).start()

    def sweep(has_left):
        gather_0()
        if has_left:
            send_first()
        gather_1()
        gather_2()
        gather_3()
        for e in range(count):
            start_copy(e).wait_recv()
            total = source_ref[e].astype(F32) + dot(s["coupled"][...], s["start"][e])
            if has_left:
                flux_copy(e).wait_recv()
                total = total + s["flux"][e].astype(F32)
            forward = green(e, total.astype(BF16))
            if e == 0:
                transpose_coupled()
            s["flux_out"][e] = dot(s["coupled_t"][...], forward).astype(BF16)
            flux_copy(e).start()
        for e in range(count):
            wave_copy(e).wait_recv()
            total = source_ref[e].astype(F32) + dot(s["coupled"][...], s["right_wave"][e])
            if has_left:
                total = total + s["flux"][e].astype(F32)
            wave_ref[e] = green(e, total.astype(BF16))
            if has_left:
                wave_copy(e).start()

    def last_sweep():
        send_first()
        for e in range(count):
            flux_copy(e).wait_recv()
            if e == 0:
                gather_0()
            total = source_ref[e].astype(F32) + s["flux"][e].astype(F32)
            wave_ref[e] = green(e, total.astype(BF16))
            wave_copy(e).start()
            if e == 0:
                gather_1()
        gather_2()

    @pl.when(slab == 0)
    def _():
        sweep(False)

    if slabs > 2:
        @pl.when((slab > 0) & (slab < slabs - 1))
        def _():
            sweep(True)

    @pl.when(slab == slabs - 1)
    def _():
        last_sweep()

    chunks = 4
    width = 2 * orbitals // chunks

    def scatter_axis(c, i):
        return ("xy", "yx")[c % 2][i]

    def scatter_place(c, i, keep):
        axis = scatter_axis(c, i)
        here = (x if axis == "x" else y) if keep else (1 - x if axis == "x" else 1 - y)
        if i == 1:
            return (slice(None), here)
        return (slice(None), slice(None), here) if axis == "x" else (slice(None), here)

    def scatter_across(c, i):
        return pltpu.make_async_remote_copy(
            src_ref=s["part"][c][i].at[scatter_place(c, i, False)], dst_ref=s["part_in"][c][i],
            send_sem=s["scatter_send"].at[c, i], recv_sem=s["scatter_recv"].at[c, i],
            device_id={"energy": across[scatter_axis(c, i)]}, device_id_type=MESH,
        )

    def scatter_layer(c, j):
        return pltpu.make_async_remote_copy(
            src_ref=s["part"][c][2].at[(z + j) % layers], dst_ref=s["part_in"][c][2].at[j],
            send_sem=s["final_send"].at[c, j], recv_sem=s["final_recv"].at[c, j],
            device_id={"energy": layer_peer(j)}, device_id_type=MESH,
        )

    scaled = []
    for e in range(count):
        index = jnp.full((1, 2 * modes), s["index"][e].astype(F32), F32)
        weight = scale / (1.0 + jnp.exp((index - 128.0) / 24.0))
        scaled.append((wave_ref[e].astype(F32) * weight).astype(BF16))
    left_side = jnp.concatenate(scaled, axis=1)
    for c in range(chunks):
        imag, quarter = c % 2, c // 2
        span = slice(quarter * width, (quarter + 1) * width)
        waves = [turned(wave_ref[e, span, :]) if imag else wave_ref[e, span, :] for e in range(count)]
        part = dot_nt(left_side, jnp.concatenate(waves, axis=1))
        s["part"][c][0][...] = part.reshape(layers, 2, 2, rows, width).astype(BF16)
        scatter_across(c, 0).start()

    @pl.when(slab == slabs - 1)
    def _():
        gather_3()
        transpose_coupled()

    for e in range(count):
        outflow_ref[e] = dot(s["coupled_t"][...], wave_ref[e]).astype(BF16)

    for i in range(2):
        for c in range(chunks):
            scatter_across(c, i).wait_recv()
            total = s["part"][c][i][scatter_place(c, i, True)].astype(F32) + s["part_in"][c][i][...].astype(F32)
            s["part"][c][i + 1][...] = total.astype(BF16)
            if i == 0:
                scatter_across(c, 1).start()
            else:
                for j in range(1, layers):
                    scatter_layer(c, j).start()
    for c in range(chunks):
        imag, quarter = c % 2, c // 2
        total = s["part"][c][2][z].astype(F32)
        for j in range(1, layers):
            scatter_layer(c, j).wait_recv()
            total = total + s["part_in"][c][2][j].astype(F32)
        begin = imag * orbitals + quarter * width
        density_ref[:, begin:begin + width] = total

    for j in range(1, layers):
        gather_layer(j).wait_send()
        for c in range(chunks):
            scatter_layer(c, j).wait_send()
    for i in range(2):
        for h in range(2):
            gather_across(h, i).wait_send()
        for c in range(chunks):
            scatter_across(c, i).wait_send()

    @pl.when(slab > 0)
    def _():
        for e in range(count):
            start_copy(e).wait_send()
            wave_copy(e).wait_send()

    @pl.when(slab < slabs - 1)
    def _():
        for e in range(count):
            flux_copy(e).wait_send()


def shards(green_local, coupling, masks, incident, energy_index):
    count = green_local.shape[0]
    orbitals = green_local.shape[3]
    modes = incident.shape[4]
    rows = coupling.shape[1]
    slabs = lax.axis_size("slab")
    n = lax.axis_size("energy")
    layers = n // 4
    chunks = 4
    width = 2 * orbitals // chunks
    wave = (count, orbitals, 2 * modes)
    dma = pltpu.SemaphoreType.DMA
    scratch = {
        "gathered": pltpu.VMEM((layers, 2, 2, rows, orbitals), BF16),
        "raw": pltpu.VMEM((count, orbitals, 2, modes), BF16),
        "source": pltpu.VMEM(wave, BF16),
        "index": pltpu.SMEM((count,), jnp.int32),
        "mask": pltpu.SMEM(masks.shape[1:], jnp.int32),
        "green": pltpu.VMEM((count, orbitals, 2 * orbitals), BF16),
        "coupled": pltpu.VMEM((orbitals, orbitals), BF16),
        "coupled_t": pltpu.VMEM((orbitals, orbitals), BF16),
        "first": pltpu.VMEM(wave, BF16),
        "flux_out": pltpu.VMEM(wave, BF16),
        "part": [[pltpu.VMEM((layers,) + (2,) * (2 - i) + (rows, width), BF16) for i in range(3)] for c in range(chunks)],
        "part_in": [[pltpu.VMEM((layers,) + (2,) * max(1 - i, 0) + (rows, width), BF16) for i in range(3)] for c in range(chunks)],
        "local": dma((4,)),
        "green_in": dma((count, 2)),
        "layer_send": dma((layers,)),
        "layer_recv": dma((layers,)),
        "across_send": dma((2, 2)),
        "across_recv": dma((2, 2)),
        "scatter_send": dma((chunks, 2)),
        "scatter_recv": dma((chunks, 2)),
        "final_send": dma((chunks, layers)),
        "final_recv": dma((chunks, layers)),
    }
    for name in ("start", "flux", "right_wave"):
        scratch[name] = pltpu.VMEM(wave, BF16)
        scratch[name + "_send"] = dma((count,))
        scratch[name + "_recv"] = dma((count,))
    vmem = pl.BlockSpec(memory_space=pltpu.VMEM)
    hbm = pl.BlockSpec(memory_space=pltpu.HBM)
    wave_field, outflow, density = pl.pallas_call(
        functools.partial(build, n, slabs, count, 4.0 / (count * n * modes)),
        out_shape=(
            jax.ShapeDtypeStruct(wave, BF16),
            jax.ShapeDtypeStruct(wave, BF16),
            jax.ShapeDtypeStruct((rows, 2 * orbitals), F32),
        ),
        in_specs=[hbm] * 5,
        out_specs=(vmem, vmem, vmem),
        scratch_shapes=[scratch],
        compiler_params=pltpu.CompilerParams(
            collective_id=0, has_side_effects=True, vmem_limit_bytes=60 * 2**20
        ),
        name="sweep_and_density",
    )(energy_index, masks, green_local, incident, coupling)
    shape = (count, 1, orbitals, 2, modes)
    return (wave_field.reshape(shape), outflow.reshape(shape), density.reshape(1, rows, 2, orbitals))


def solution(mesh):
    return jax.shard_map(
        shards,
        mesh=mesh,
        in_specs=(
            P("energy", "slab", None, None, None),
            P("slab", "energy", None),
            P("slab", None, None),
            P("energy", "slab", None, None, None),
            P("energy"),
        ),
        out_specs=(
            P("energy", "slab", None, None, None),
            P("energy", "slab", None, None, None),
            P("slab", "energy", None, None),
        ),
        check_vma=False,
    )
```

time: 54.6 us -> 52.2 us (0.956)
  local copies, waits for them, and re-layouts: 7.65 us -> 5.58 us
    unnamed x8 -> x0, local copies, waits for them, and re-layouts: 3.68 us -> none
    another operation x1 -> x0, local copies, waits for them, and re-layouts: 1.37 us -> none  [shards(): incident[:, 0].reshape(wave)]
    reshape x1, local copies, waits for them, and re-layouts: 0.92 us -> 1.96 us  [shards(): wave_field.reshape(shape)]
    reshape x1, local copies, waits for them, and re-layouts: 0.92 us -> 1.96 us  [shards(): outflow.reshape(shape)]
    reshape x1, local copies, waits for them, and re-layouts: 0.76 us -> 1.67 us  [shards(): density.reshape(1, rows, 2, orbitals)]
where the time goes in v2:
time: 52.2 us; the launch traced here: 52 us
  Pallas kernels  45.7 us (88%)
  local copies, waits for them, and re-layouts  5.58 us (11%)
  between operations  0.64 us (1%)
    pallas_call x1, Pallas kernels, shards(): pl.pallas_call(functools.partial(build, n, slabs, count, 4.0 / (count * n...  45.7 us
    reshape x1, local copies, waits for them, and re-layouts, shards(): wave_field.reshape(shape)  1.96 us
    reshape x1, local copies, waits for them, and re-layouts, shards(): outflow.reshape(shape)  1.96 us
    reshape x1, local copies, waits for them, and re-layouts, shards(): density.reshape(1, rows, 2, orbitals)  1.67 us

profile of v2, /device:TPU:0, one launch (start us, length us, event | category | flops | bytes accessed | tf_op | source)
XLA Modules:
  0.0 52.0 jit_solution(5642378799242012714)
XLA Ops:
  0.6 45.7 %sweep_and_density.1 = (bf16[2,512,256]{2,1,0:T(8,128)(2,1)}, bf16[2,512,256]{2,1,0:T(8,128)(2,1)}, f32[32,1024]{1,0:T(8,128)}) custom-call(s32[2]{0:T(128)} %index_hbm.1, s32[1,4,4]{2,1,0:T(4,128)} %mask_hbm.1, bf16[2,1,2,512,512]{4,3,2,1,0:T(8,128)(2,1)} %green_hbm.1, bf16[2,1,512,2,128]{4,3,2,1,0:T(2,128)(2,1)} %incident_hbm.1, ...), custom_call_target="tpu_custom_call" | custom-call | tf_op jit(solution)/shard_map/sweep_and_density/pallas_call | solution.py:336
  46.4 2.0 %reshape.15 = bf16[2,1,512,2,128]{4,3,2,0,1:T(2,128)(2,1)} reshape(bf16[2,512,256]{2,1,0:T(8,128)(2,1)} %get-tuple-element.6) | data formatting | bytes 1048576 | tf_op jit(solution)/shard_map/reshape | solution.py:352
  48.3 1.7 %reshape.17 = f32[1,32,2,512]{3,2,1,0:T(2,128)} reshape(f32[32,1024]{1,0:T(8,128)} %get-tuple-element.8) | data formatting | bytes 262144 | tf_op jit(solution)/shard_map/reshape | solution.py:352
  50.0 2.0 %reshape.16 = bf16[2,1,512,2,128]{4,3,2,0,1:T(2,128)(2,1)} reshape(bf16[2,512,256]{2,1,0:T(8,128)(2,1)} %get-tuple-element.7) | data formatting | bytes 1048576 | tf_op jit(solution)/shard_map/reshape | solution.py:352

commit v3 on v2

--- a/solution.py
+++ b/solution.py
@@ -68,13 +68,17 @@
     def _():
         pl.semaphore_signal(barrier, inc=1, device_id={"slab": slab + 1}, device_id_type=MESH)
 
-    local[1].wait()
-    for e in range(count):
-        source_ref[e] = jnp.concatenate([s["raw"][e, :, 0, :], s["raw"][e, :, 1, :]], axis=1)
-    for copy in [local[0]] + local[2:] + green_copies:
-        copy.wait()
+    local[0].wait()
     neighbours = jnp.minimum(slab, 1) + jnp.minimum(slabs - 1 - slab, 1)
     pl.semaphore_wait(barrier, layers + 1 + neighbours)
+
+    def load():
+        for copy in local[1:]:
+            copy.wait()
+        for e in range(count):
+            source_ref[e] = jnp.concatenate([s["raw"][e, :, 0, :], s["raw"][e, :, 1, :]], axis=1)
+        for copy in green_copies:
+            copy.wait()
 
     def green(e, v):
         return dot(s["green"][e], jnp.concatenate([v, turned(v)], axis=0)).astype(BF16)
@@ -151,8 +155,11 @@
     def sweep(has_left):
         gather_0()
         if has_left:
+            load()
             send_first()
         gather_1()
+        if not has_left:
+            load()
         gather_2()
         gather_3()
         for e in range(count):
@@ -176,6 +183,7 @@
                 wave_copy(e).start()
 
     def last_sweep():
+        load()
         send_first()
         for e in range(count):
             flux_copy(e).wait_recv()
@@ -336,9 +344,9 @@
     wave_field, outflow, density = pl.pallas_call(
         functools.partial(build, n, slabs, count, 4.0 / (count * n * modes)),
         out_shape=(
-            jax.ShapeDtypeStruct(wave, BF16),
-            jax.ShapeDtypeStruct(wave, BF16),
-            jax.ShapeDtypeStruct((rows, 2 * orbitals), F32),
+            pltpu.VMEM(wave, BF16),
+            pltpu.VMEM(wave, BF16),
+            pltpu.VMEM((rows, 2 * orbitals), F32),
         ),
         in_specs=[hbm] * 5,
         out_specs=(vmem, vmem, vmem),

time: 52.2 us -> 47.9 us (0.918)
  local copies, waits for them, and re-layouts: 5.58 us -> 2.6 us
  Pallas kernels: 45.7 us -> 44.5 us
    pallas_call x1, Pallas kernels: 45.7 us -> 44.5 us  [shards(): pl.pallas_call(functools.partial(build, n, slabs, count, 4.0 / (count * n...]
    reshape x1, local copies, waits for them, and re-layouts: 1.96 us -> 0.92 us  [shards(): wave_field.reshape(shape)]
    reshape x1, local copies, waits for them, and re-layouts: 1.96 us -> 0.92 us  [shards(): outflow.reshape(shape)]
    reshape x1, local copies, waits for them, and re-layouts: 1.67 us -> 0.76 us  [shards(): density.reshape(1, rows, 2, orbitals)]
where the time goes in v3:
time: 47.9 us; the launch traced here: 47.8 us
  Pallas kernels  44.5 us (93%)
  local copies, waits for them, and re-layouts  2.6 us (5%)
  between operations  0.64 us (1%)
    pallas_call x1, Pallas kernels, shards(): pl.pallas_call(functools.partial(build, n, slabs, count, 4.0 / (count * n...  44.5 us

profile of v3, /device:TPU:0, one launch (start us, length us, event | category | flops | bytes accessed | tf_op | source)
XLA Modules:
  0.0 47.8 jit_solution(17319182113745460569)
XLA Ops:
  0.6 44.5 %sweep_and_density.1 = (bf16[2,512,256]{2,1,0:T(8,128)(2,1)S(1)}, bf16[2,512,256]{2,1,0:T(8,128)(2,1)S(1)}, f32[32,1024]{1,0:T(8,128)S(1)}) custom-call(s32[2]{0:T(128)} %index_hbm.1, s32[1,4,4]{2,1,0:T(4,128)} %mask_hbm.1, bf16[2,1,2,512,512]{4,3,2,1,0:T(8,128)(2,1)} %green_hbm.1, bf16[2,1,512,2,128]{4,3,2,1,0:T(2,128)(2,1)} %incident_hbm.1, ...), custom_call_target="tpu_custom_call" | custom-call | tf_op jit(solution)/shard_map/sweep_and_density/pallas_call | solution.py:344
  45.2 0.9 %reshape.15 = bf16[2,1,512,2,128]{4,3,2,0,1:T(2,128)(2,1)} reshape(bf16[2,512,256]{2,1,0:T(8,128)(2,1)S(1)} %get-tuple-element.6) | data formatting | bytes 1048576 | tf_op jit(solution)/shard_map/reshape | solution.py:360
  46.1 0.8 %reshape.17 = f32[1,32,2,512]{3,2,1,0:T(2,128)} reshape(f32[32,1024]{1,0:T(8,128)S(1)} %get-tuple-element.8) | data formatting | bytes 262144 | tf_op jit(solution)/shard_map/reshape | solution.py:360
  46.8 0.9 %reshape.16 = bf16[2,1,512,2,128]{4,3,2,0,1:T(2,128)(2,1)} reshape(bf16[2,512,256]{2,1,0:T(8,128)(2,1)S(1)} %get-tuple-element.7) | data formatting | bytes 1048576 | tf_op jit(solution)/shard_map/reshape | solution.py:360

commit v4 on v3

--- a/solution.py
+++ b/solution.py
@@ -23,6 +23,26 @@
 def turned(x):
     half = x.shape[1] // 2
     return jnp.concatenate([-x[:, half:], x[:, :half]], axis=1)
+
+
+PIECES = 4
+
+
+class Group:
+    def __init__(self, copies):
+        self.copies = copies
+
+    def start(self):
+        for copy in self.copies:
+            copy.start()
+
+    def wait_recv(self):
+        for copy in self.copies:
+            copy.wait_recv()
+
+    def wait_send(self):
+        for copy in self.copies:
+            copy.wait_send()
 
 
 def build(n, slabs, count, scale, index_hbm, mask_hbm, green_hbm, incident_hbm, coupling_hbm,
@@ -72,23 +92,29 @@
     neighbours = jnp.minimum(slab, 1) + jnp.minimum(slabs - 1 - slab, 1)
     pl.semaphore_wait(barrier, layers + 1 + neighbours)
 
-    def load():
-        for copy in local[1:]:
-            copy.wait()
-        for e in range(count):
+    def load(energies):
+        if 0 in energies:
+            for copy in local[1:]:
+                copy.wait()
+        for e in energies:
             source_ref[e] = jnp.concatenate([s["raw"][e, :, 0, :], s["raw"][e, :, 1, :]], axis=1)
-        for copy in green_copies:
-            copy.wait()
+            for p in range(2):
+                green_copies[2 * e + p].wait()
 
     def green(e, v):
         return dot(s["green"][e], jnp.concatenate([v, turned(v)], axis=0)).astype(BF16)
 
     def slab_copy(name, e, src, target):
-        return pltpu.make_async_remote_copy(
-            src_ref=src.at[e], dst_ref=s[name].at[e],
-            send_sem=s[name + "_send"].at[e], recv_sem=s[name + "_recv"].at[e],
-            device_id={"slab": target}, device_id_type=MESH,
-        )
+        height = orbitals // PIECES
+        copies = []
+        for q in range(PIECES):
+            span = pl.ds(q * height, height)
+            copies.append(pltpu.make_async_remote_copy(
+                src_ref=src.at[e, span], dst_ref=s[name].at[e, span],
+                send_sem=s[name + "_send"].at[e, q], recv_sem=s[name + "_recv"].at[e, q],
+                device_id={"slab": target}, device_id_type=MESH,
+            ))
+        return Group(copies)
 
     def start_copy(e):
         return slab_copy("start", e, s["first"], slab - 1)
@@ -149,18 +175,20 @@
 
     def send_first():
         for e in range(count):
+            load([e])
             s["first"][e] = green(e, source_ref[e])
             start_copy(e).start()
 
     def sweep(has_left):
         gather_0()
         if has_left:
-            load()
             send_first()
+        else:
+            load(range(1))
         gather_1()
+        gather_2()
         if not has_left:
-            load()
-        gather_2()
+            load(range(1, count))
         gather_3()
         for e in range(count):
             start_copy(e).wait_recv()
@@ -183,7 +211,6 @@
                 wave_copy(e).start()
 
     def last_sweep():
-        load()
         send_first()
         for e in range(count):
             flux_copy(e).wait_recv()
@@ -192,9 +219,7 @@
             total = source_ref[e].astype(F32) + s["flux"][e].astype(F32)
             wave_ref[e] = green(e, total.astype(BF16))
             wave_copy(e).start()
-            if e == 0:
-                gather_1()
-        gather_2()
+        gather_1()
 
     @pl.when(slab == 0)
     def _():
@@ -250,13 +275,17 @@
         s["part"][c][0][...] = part.reshape(layers, 2, 2, rows, width).astype(BF16)
         scatter_across(c, 0).start()
 
+    def outflow():
+        for e in range(count):
+            outflow_ref[e] = dot(s["coupled_t"][...], wave_ref[e]).astype(BF16)
+
+    @pl.when(slab < slabs - 1)
+    def _():
+        outflow()
+
     @pl.when(slab == slabs - 1)
     def _():
-        gather_3()
-        transpose_coupled()
-
-    for e in range(count):
-        outflow_ref[e] = dot(s["coupled_t"][...], wave_ref[e]).astype(BF16)
+        gather_2()
 
     for i in range(2):
         for c in range(chunks):
@@ -268,6 +297,13 @@
             else:
                 for j in range(1, layers):
                     scatter_layer(c, j).start()
+
+    @pl.when(slab == slabs - 1)
+    def _():
+        gather_3()
+        transpose_coupled()
+        outflow()
+
     for c in range(chunks):
         imag, quarter = c % 2, c // 2
         total = s["part"][c][2][z].astype(F32)
@@ -337,8 +373,8 @@
     }
     for name in ("start", "flux", "right_wave"):
         scratch[name] = pltpu.VMEM(wave, BF16)
-        scratch[name + "_send"] = dma((count,))
-        scratch[name + "_recv"] = dma((count,))
+        scratch[name + "_send"] = dma((count, PIECES))
+        scratch[name + "_recv"] = dma((count, PIECES))
     vmem = pl.BlockSpec(memory_space=pltpu.VMEM)
     hbm = pl.BlockSpec(memory_space=pltpu.HBM)
     wave_field, outflow, density = pl.pallas_call(

time: 47.9 us -> 46.1 us (0.962)
  Pallas kernels: 44.5 us -> 42.7 us
    pallas_call x1, Pallas kernels: 44.5 us -> 42.7 us  [shards(): pl.pallas_call(functools.partial(build, n, slabs, count, 4.0 / (count * n...]
where the time goes in v4:
time: 46.1 us; the launch traced here: 46 us
  Pallas kernels  42.7 us (93%)
  local copies, waits for them, and re-layouts  2.6 us (6%)
  between operations  0.64 us (1%)
    pallas_call x1, Pallas kernels, shards(): pl.pallas_call(functools.partial(build, n, slabs, count, 4.0 / (count * n...  42.7 us

profile of v4, /device:TPU:0, one launch (start us, length us, event | category | flops | bytes accessed | tf_op | source)
XLA Modules:
  0.0 46.0 jit_solution(3141875086023064377)
XLA Ops:
  0.6 42.7 %sweep_and_density.1 = (bf16[2,512,256]{2,1,0:T(8,128)(2,1)S(1)}, bf16[2,512,256]{2,1,0:T(8,128)(2,1)S(1)}, f32[32,1024]{1,0:T(8,128)S(1)}) custom-call(s32[2]{0:T(128)} %index_hbm.1, s32[1,4,4]{2,1,0:T(4,128)} %mask_hbm.1, bf16[2,1,2,512,512]{4,3,2,1,0:T(8,128)(2,1)} %green_hbm.1, bf16[2,1,512,2,128]{4,3,2,1,0:T(2,128)(2,1)} %incident_hbm.1, ...), custom_call_target="tpu_custom_call" | custom-call | tf_op jit(solution)/shard_map/sweep_and_density/pallas_call | solution.py:380
  43.4 0.9 %reshape.15 = bf16[2,1,512,2,128]{4,3,2,0,1:T(2,128)(2,1)} reshape(bf16[2,512,256]{2,1,0:T(8,128)(2,1)S(1)} %get-tuple-element.6) | data formatting | bytes 1048576 | tf_op jit(solution)/shard_map/reshape | solution.py:396
  44.3 0.8 %reshape.17 = f32[1,32,2,512]{3,2,1,0:T(2,128)} reshape(f32[32,1024]{1,0:T(8,128)S(1)} %get-tuple-element.8) | data formatting | bytes 262144 | tf_op jit(solution)/shard_map/reshape | solution.py:396
  45.1 0.9 %reshape.16 = bf16[2,1,512,2,128]{4,3,2,0,1:T(2,128)(2,1)} reshape(bf16[2,512,256]{2,1,0:T(8,128)(2,1)S(1)} %get-tuple-element.7) | data formatting | bytes 1048576 | tf_op jit(solution)/shard_map/reshape | solution.py:396
